TPU v7x, 32 devices: a whole 2x2x4 slice. The times are simulated.
32 devices in a mesh: tile: 4 (over z), focus: 8 (over y, x, core).
Axes of the slice: x: 2, y: 2, z: 4, core: 2. Of those that a mesh axis runs over, the one named last changes fastest.
Arguments:
- mask_tiles: bfloat16 [256, 512, 512], P(('tile', 'focus')), may hold values from -1 to 1
- class_of_tile: int32 [256, 1], P(('tile', 'focus')), may hold values from 0 to 7; in each aligned block of 8 rows (0 to 7, 8 to 15, ...) at most 2 rows name the same one
- cell_of_tile: int32 [256], P(('tile', 'focus')), may hold values from 0 to 511
- kernels: bfloat16 [8, 24, 4, 4096], P('focus'), may hold values from -0.19921875 to 0.19921875
- class_center: float32 [8], replicated, may hold values from -0.6 to 0.6
Outputs:
- resist_image: bfloat16 [256, 512, 512], P(('tile', 'focus'))
Inputs may be any that keep to these rules, and one draw needn't show every extreme that they name: `class_of_tile`: the 8 tiles of one device hold at most 2 tiles of any one class.
All inputs are finite; a program needn't handle non-finite values.
Results may differ from a plain program's by a relative error of at most 0.009.
Values may be sent and summed in bfloat16 or wider, within the bound.
A program may use at most 128 MiB of HBM per device.

v0:
```python
import jax
import jax.numpy as jnp
from jax import lax
from jax.sharding import PartitionSpec as P

P_SIZE = 512
NF = 64
KER = 24
BLK_PX = 64
CAP = 2
SC = 32
SR_DEV = 4
Q = 128
B = 8
REACH = 64


GAIN_SCALE = 50.0
BEST = lax.Precision.HIGHEST


def for_sending(x):

    def short(part):
        return part.astype(jnp.bfloat16) if part.dtype == jnp.float32 else part

    return jax.tree.map(short, x)


def spectral_table(freq_count, length):
    frequency = jnp.arange(freq_count, dtype=jnp.int32) - freq_count // 2
    places = jnp.arange(length, dtype=jnp.int32)
    phases = jnp.mod(frequency[:, None] * places[None, :], length).astype(jnp.float32) * (
        2.0 * jnp.pi / length
    )
    return (jnp.cos(phases), jnp.sin(phases))


def imaging_table(freq_count, samples):
    cosine, sine_part = spectral_table(freq_count, samples)
    upper_rows = jnp.concatenate([cosine, sine_part], axis=1)
    lower_rows = jnp.concatenate([-sine_part, cosine], axis=1)
    return jnp.concatenate([upper_rows, lower_rows], axis=0).astype(jnp.bfloat16)


def resist_table(pixels, samples):
    cos_pix, sin_pix = spectral_table(samples, pixels)
    cos_smp, sin_smp = spectral_table(samples, samples)
    frequency = (jnp.arange(samples, dtype=jnp.int32) - samples // 2).astype(jnp.float32)
    weight = jnp.exp(-0.5 * (frequency * (4.0 / samples)) ** 2)
    combined = jnp.dot((cos_pix * weight[:, None]).T, cos_smp, precision=BEST)
    combined = combined + jnp.dot((sin_pix * weight[:, None]).T, sin_smp, precision=BEST)
    return (combined / samples).astype(jnp.bfloat16)


def spread_table(extent, length):
    places = jnp.arange(extent, dtype=jnp.int32).astype(jnp.float32)
    weight = jnp.exp(-jnp.abs(places[:, None] - places[None, :]) / length)
    return weight / jnp.sum(weight, axis=1, keepdims=True)


def to_map(totals):
    strips = totals.shape[0] // SC
    return totals.reshape(strips, SC, B, B).transpose(0, 2, 1, 3).reshape(strips * B, SC * B)


def cell_means(field_map):
    strips = field_map.shape[0] // B
    return jnp.mean(field_map.reshape(strips, B, SC, B), axis=(1, 3)).reshape(strips * SC)


def split_spectrum(raw_spectrum):
    cos_cos = raw_spectrum[..., :NF, :NF]
    cos_sin = raw_spectrum[..., :NF, NF:]
    sin_cos = raw_spectrum[..., NF:, :NF]
    sin_sin = raw_spectrum[..., NF:, NF:]
    real_part = (cos_cos - sin_sin) / P_SIZE
    imag_part = -(cos_sin + sin_cos) / P_SIZE
    stacked = jnp.stack([real_part, imag_part], axis=-3)
    return stacked.reshape(raw_spectrum.shape[:-2] + (2, NF * NF)).astype(jnp.bfloat16)


def image_one(spectrum, defocus, kernel_set, right_table, left_table):
    spec_parts = spectrum.astype(jnp.float32)
    weights = kernel_set.astype(jnp.float32)
    kern_re = weights[:, 0] + defocus * weights[:, 2]
    kern_im = weights[:, 1] + defocus * weights[:, 3]
    prod_re = kern_re * spec_parts[0] - kern_im * spec_parts[1]
    prod_im = kern_re * spec_parts[1] + kern_im * spec_parts[0]
    stacked = jnp.concatenate([prod_re.reshape(KER, NF, NF), prod_im.reshape(KER, NF, NF)], axis=2)
    stacked = stacked.astype(jnp.bfloat16).reshape(KER * NF, 2 * NF)
    across = jnp.dot(stacked, right_table, preferred_element_type=jnp.float32).astype(jnp.bfloat16)
    across = across.reshape(KER, NF, 2 * Q)
    fields = jnp.einsum(
        "pu,kuv->pkv", left_table[:, :NF], across[:, :, :Q], preferred_element_type=jnp.float32
    )
    fields = fields + jnp.einsum(
        "pu,kuv->pkv", left_table[:, NF:], across[:, :, Q:], preferred_element_type=jnp.float32
    )
    return jnp.sum((fields * fields).reshape(2, Q, KER, Q), axis=(0, 2)).reshape(Q * Q) / KER


def per_device(mask_tiles, class_of_tile, cell_of_tile, kernels, class_center):
    tile_count = mask_tiles.shape[0]
    wave_rows = jnp.concatenate(spectral_table(NF, P_SIZE), axis=0).astype(jnp.bfloat16)
    projected = jnp.dot(
        mask_tiles.reshape(tile_count * P_SIZE, P_SIZE),
        wave_rows.T,
        preferred_element_type=jnp.float32,
    )
    projected = projected.astype(jnp.bfloat16).reshape(tile_count, P_SIZE, 2 * NF)
    raw_spectrum = jnp.einsum(
        "ux,txv->tuv", wave_rows, projected, preferred_element_type=jnp.float32
    )
    spectra = split_spectrum(raw_spectrum)
    squares = mask_tiles.astype(jnp.float32) ** 2
    density = jnp.sum(squares.reshape(tile_count, B, BLK_PX, B, BLK_PX), axis=(2, 4)) / (
        BLK_PX * BLK_PX
    )
    cell_count = SR_DEV * lax.axis_size("tile") * SC
    owner_cells = (
        jnp.arange(cell_count, dtype=jnp.int32)[:, None] == cell_of_tile[None, :]
    ).astype(jnp.float32)
    partial_value = jnp.dot(owner_cells, density.reshape(tile_count, B * B), precision=BEST)
    totals = lax.psum(partial_value, ("tile", "focus"))
    density_map = to_map(totals)
    effective = jnp.dot(spread_table(density_map.shape[0], REACH), density_map, precision=BEST)
    effective = jnp.dot(effective, spread_table(density_map.shape[1], REACH), precision=BEST)
    heights = cell_means(effective)
    classes = class_of_tile[:, 0]
    set_count = kernels.shape[0] * lax.axis_size("focus")
    class_hot = classes[:, None] == jnp.arange(set_count, dtype=jnp.int32)[None, :]
    centre = jnp.sum(jnp.where(class_hot, class_center[None, :], 0.0), axis=1)
    own_height = jnp.dot(heights, owner_cells, precision=BEST)
    defocus = GAIN_SCALE * (own_height - jnp.mean(heights)) - centre
    right_table = imaging_table(NF, Q)
    left_table = right_table.T
    class_int = class_hot.astype(jnp.int32)
    before = jnp.cumsum(class_int, axis=0) - class_int
    slot_ids = jnp.sum(before * class_int, axis=1) + classes * CAP
    placed = jnp.arange(set_count * CAP, dtype=jnp.int32)[:, None] == slot_ids[None, :]
    outgoing = jnp.dot(
        placed.astype(jnp.bfloat16),
        spectra.reshape(tile_count, 2 * NF * NF),
        preferred_element_type=jnp.float32,
    )
    outgoing = outgoing.astype(jnp.bfloat16).reshape(set_count, CAP, 2 * NF * NF)
    out_shift = jnp.dot(placed.astype(jnp.float32), defocus, precision=BEST).reshape(set_count, CAP)
    own_kernels = kernels[0]
    got_spectra = lax.all_to_all(outgoing, "focus", split_axis=0, concat_axis=0, tiled=True)
    got_shift = lax.all_to_all(
        out_shift.astype(jnp.bfloat16), "focus", split_axis=0, concat_axis=0, tiled=True
    ).astype(out_shift.dtype)
    sources = got_spectra.shape[0]
    slots_each = got_spectra.shape[1]
    flat_spectra = got_spectra.reshape(sources * slots_each, 2, NF * NF)
    lit_slots = lax.map(
        lambda single: image_one(single[0], single[1], own_kernels, right_table, left_table),
        (flat_spectra, got_shift.reshape(sources * slots_each)),
        batch_size=2 * CAP,
    )
    returned = lax.all_to_all(
        for_sending(lit_slots.reshape(sources, slots_each, Q * Q)),
        "focus",
        split_axis=0,
        concat_axis=0,
        tiled=True,
    )
    intensity = jnp.dot(
        placed.astype(jnp.float32).T, returned.reshape(set_count * CAP, Q * Q), precision=BEST
    )
    resist_rows = resist_table(P_SIZE, Q)
    light_rows = intensity.astype(jnp.bfloat16).reshape(tile_count * Q, Q)
    half_way = jnp.dot(light_rows, resist_rows.T, preferred_element_type=jnp.float32)
    half_way = half_way.astype(jnp.bfloat16).reshape(tile_count, Q, P_SIZE)
    return jnp.einsum(
        "xq,tqy->txy", resist_rows, half_way, preferred_element_type=jnp.float32
    ).astype(jnp.bfloat16)


def solution(mesh):
    placed = (
        P(("tile", "focus"), None, None),
        P(("tile", "focus"), None),
        P(("tile", "focus")),
        P("focus", None, None, None),
        P(),
    )
    return jax.shard_map(
        per_device,
        mesh=mesh,
        in_specs=placed,
        out_specs=P(("tile", "focus"), None, None),
        check_vma=False,
    )
```

profile of v0, /device:TPU:0, one launch (start us, length us, event | category | flops | bytes accessed | tf_op | source)
XLA Modules:
  0.0 279.2 jit_solution(15670433752014647923)
XLA Ops:
  6.5 6.6 %convert_multiply_fusion = f32[8,512,512]{2,1,0:T(8,128)} fusion(bf16[8,512,512]{2,1,0:T(8,128)(2,1)} %param.7), kind=kLoop, calls=%fused_computation.33 | loop fusion | flops 4194304 | bytes 12582912 | tf_op jit(solution)/shard_map/integer_pow | solution.py:116
  13.1 12.9 %reshape.184 = f32[8,8,64,8,64]{4,3,2,1,0:T(8,128)} reshape(f32[8,512,512]{2,1,0:T(8,128)} %convert_multiply_fusion) | data formatting | bytes 16777216 | tf_op jit(solution)/shard_map/reshape | solution.py:117
  26.0 7.0 %reduce_sum.83 = f32[8,8,8]{2,1,0:T(8,128)S(1)} reduce(f32[8,8,64,8,64]{4,3,2,1,0:T(8,128)} %reshape.184, f32[]{:T(128)} %constant.92.clone.1), dimensions={2,4}, to_apply=%region_3.4 | reduce | flops 2096640 | bytes 8390660 | tf_op jit(solution)/shard_map/reduce_sum | solution.py:117
  34.2 1.9 reshape.186
  37.0 3.7 %convolution_convert_fusion.3 = bf16[128,4096]{1,0:T(8,128)(2,1)S(1)} fusion(bf16[4096,512]{1,0:T(8,128)(2,1)} %bitcast.135, bf16[64,512]{1,0:T(8,128)(2,1)S(1)} %get-tuple-element.103, bf16[64,512]{1,0:T(8,128)(2,1)S(1)} %get-tuple-element.102), kind=kOutput, calls=%fused_computation.34 | convolution fusion | flops 537657344 | bytes 5373952 | tf_op jit(solution)/shard_map/dot_general | solution.py:106
  44.0 117.4 %all-reduce.2.cloned.1.call-done = f32[128,256]{1,0:T(8,128)} async-done(((f32[128,256]{1,0:T(8,128)}), f32[128,256]{1,0:T(8,128)}) %all-reduce.2.cloned.1.call-update) | async-done | bytes 131088 | tf_op jit(solution)/shard_map/psum | solution.py:125
  166.3 8.1 %all_to_all.16 = bf16[8,1,2]{2,1,0:T(2,128)(2,1)S(1)} all-to-all(bf16[8,1,2]{2,1,0:T(2,128)(2,1)S(1)} %convert_element_type.166), channel_id=1, replica_groups=mesh['tile'=4,'focus'=8] {'focus'}, dimensions={0} | all-to-all | bytes 64 | tf_op jit(solution)/shard_map/all_to_all | solution.py:151
  174.4 3.6 %all-to-all-start.1 = ((bf16[8,2,8192]{2,1,0:T(2,128)(2,1)}), bf16[8,2,8192]{2,1,0:T(2,128)(2,1)S(1)}, u32[]{:S(2)}, u32[]{:S(2)}) async-start(bf16[8,2,8192]{2,1,0:T(2,128)(2,1)} %reshape.190), calls=%async_computation.1 | async-start | bytes 524288 | tf_op jit(solution)/shard_map/all_to_all | solution.py:150
  179.3 5.5 %all-to-all-done.1 = bf16[8,2,8192]{2,1,0:T(2,128)(2,1)S(1)} async-done(((bf16[8,2,8192]{2,1,0:T(2,128)(2,1)}), bf16[8,2,8192]{2,1,0:T(2,128)(2,1)S(1)}, u32[]{:S(2)}, u32[]{:S(2)}) %all-to-all-start.1) | async-done | bytes 262176 | tf_op jit(solution)/shard_map/all_to_all | solution.py:150
  185.6 60.4 %while.10 = (s32[]{:T(128)}, bf16[4,4,16384]{2,1,0:T(4,128)(2,1)}, bf16[24,4,4096]{2,0,1:T(8,128)(2,1)S(1)}, f32[4,4]{1,0:T(4,128)S(1)}, bf16[4,4,2,4096]{3,2,1,...) while((s32[]{:T(128)}, bf16[4,4,16384]{2,1,0:T(4,128)(2,1)}, ...), condition=%wide.region_12.13_spmd, body=%wide.region_9.12_spmd.sunk | while | flops 1226932224 | bytes 47383248 | solution.py:157
  189.7 1.3 mul.615
  192.2 2.7 fusion.149
  196.0 1.8 fusion.150
  197.8 1.8 multiply_reduce_fusion.2
  207.3 2.7 fusion.149
  211.1 1.8 fusion.150
  212.9 1.8 multiply_reduce_fusion.2
  219.9 1.3 mul.615
  222.4 2.7 fusion.149
  226.2 1.8 fusion.150
  228.0 1.8 multiply_reduce_fusion.2
  235.0 1.3 mul.615
  237.5 2.7 fusion.149
  241.3 1.8 fusion.150
  243.2 1.8 multiply_reduce_fusion.2
  246.0 2.4 convert_element_type.155
  248.4 3.7 %all-to-all-start.2 = ((bf16[8,2,16384]{2,1,0:T(2,128)(2,1)}), bf16[8,2,16384]{2,1,0:T(2,128)(2,1)S(1)}, u32[]{:S(2)}, u32[]{:S(2)}) async-start(bf16[8,2,16384]{2,1,0:T(2,128)(2,1)} %convert_element_type.155), calls=%async_computation.2 | async-start | bytes 1048576 | tf_op jit(solution)/shard_map/all_to_all | solution.py:162
  252.2 1.8 fusion.37
  254.0 1.8 fusion.19
  255.7 5.9 %all-to-all-done.2 = bf16[8,2,16384]{2,1,0:T(2,128)(2,1)S(1)} async-done(((bf16[8,2,16384]{2,1,0:T(2,128)(2,1)}), bf16[8,2,16384]{2,1,0:T(2,128)(2,1)S(1)}, u32[]{:S(2)}, u32[]{:S(2)}) %all-to-all-start.2) | async-done | bytes 524320 | tf_op jit(solution)/shard_map/all_to_all | solution.py:162
  262.7 3.2 %convert_bitcast_fusion = bf16[8,512,512]{1,2,0:T(8,128)(2,1)} fusion(bf16[8,128,512]{2,1,0:T(8,128)(2,1)S(1)} %bitcast.137, bf16[512,128]{1,0:T(8,128)(2,1)S(1)} %fusion.19), kind=kOutput, calls=%fused_computation.35 | convolution fusion | flops 538968064 | bytes 5373952 | tf_op jit(solution)/shard_map/xq,tqy->txy/dot_general | solution.py:176
  265.9 6.4 %copy.45 = bf16[8,512,512]{2,1,0:T(8,128)(2,1)} copy(bf16[8,512,512]{1,2,0:T(8,128)(2,1)} %convert_bitcast_fusion) | data formatting | bytes 8388608 | tf_op jit(solution)/shard_map/convert_element_type | solution.py:178
  (138 shorter events, 43.2 us)
Async XLA Ops:
  6.5 154.9 %all-reduce.2.cloned.1.call-start = ((), (), s32[]{:S(2)}) async-start(), calls=%async_computation.3 | async-start | bytes 262144 | tf_op jit(solution)/shard_map/psum | solution.py:125
  26.0 7.1 %copy-start.4 = (s32[8]{0:T(128)S(1)}, s32[8]{0:T(128)}, u32[]{:S(2)}) copy-start(s32[8]{0:T(128)} %param.9) | copy-start | bytes 100
  40.6 1.3 copy-start.3
  40.6 3.1 %copy-start.5 = (f32[8]{0:T(128)S(1)}, f32[8]{0:T(128)}, u32[]{:S(2)}) copy-start(f32[8]{0:T(128)} %param.11) | copy-start | bytes 100
  162.7 15.4 %copy-start.2 = (bf16[1,24,4,4096]{3,2,1,0:T(4,128)(2,1)S(1)}, bf16[1,24,4,4096]{3,2,1,0:T(4,128)(2,1)}, u32[]{:S(2)}) copy-start(bf16[1,24,4,4096]{3,2,1,0:T(4,128)(2,1)} %param.10) | copy-start | bytes 2359300
  174.4 10.3 %all-to-all-start.1 = ((bf16[8,2,8192]{2,1,0:T(2,128)(2,1)}), bf16[8,2,8192]{2,1,0:T(2,128)(2,1)S(1)}, u32[]{:S(2)}, u32[]{:S(2)}) async-start(bf16[8,2,8192]{2,1,0:T(2,128)(2,1)} %reshape.190), calls=%async_computation.1 | async-start | bytes 524288 | tf_op jit(solution)/shard_map/all_to_all | solution.py:150
  192.2 2.7 copy-start.1
  194.9 1.1 copy-start
  207.3 2.7 copy-start.1
  210.0 1.1 copy-start
  222.4 2.7 copy-start.1
  225.1 1.1 copy-start
  237.5 2.7 copy-start.1
  240.2 1.1 copy-start
  248.4 13.2 %all-to-all-start.2 = ((bf16[8,2,16384]{2,1,0:T(2,128)(2,1)}), bf16[8,2,16384]{2,1,0:T(2,128)(2,1)S(1)}, u32[]{:S(2)}, u32[]{:S(2)}) async-start(bf16[8,2,16384]{2,1,0:T(2,128)(2,1)} %convert_element_type.155), calls=%async_computation.2 | async-start | bytes 1048576 | tf_op jit(solution)/shard_map/all_to_all | solution.py:162
Sparse Core Ops, SparseCore 0:
  36.2 125.1 all-reduce.1
where the time goes:
time: 281 us; the launch traced here: 279 us
  waiting for transfers between devices  129 us (46%)
  local copies, waits for them, and re-layouts  58.8 us (21%)
  matrix products  33.1 us (12%)
  other arithmetic  28.3 us (10%)
  between operations  14.3 us (5%)
  blocking collectives  8.08 us (3%)
  starting transfers between devices  7.31 us (3%)
    psum x1, waiting for transfers between devices, per_device(): totals = lax.psum(partial_value, ('tile', 'focus'))  117 us
    reshape x1, local copies, waits for them, and re-layouts, per_device(): squares.reshape(tile_count, B, BLK_PX, B, BLK_PX)  12.9 us
    another operation x7, other arithmetic  11.7 us
    all_to_all x1, blocking collectives, per_device(): lax.all_to_all(out_shift.astype(jnp.bfloat16), 'focus', split_axis=0, con...  8.08 us
    dot_general x4, matrix products, image_one(): jnp.einsum('pu,kuv->pkv', left_table[:, NF:], across[:, :, Q:], preferred...  7.37 us
    dot_general x4, matrix products, image_one(): jnp.einsum('pu,kuv->pkv', left_table[:, :NF], across[:, :, :Q], preferred...  7.35 us
    reduce_sum x1, other arithmetic, per_device(): jnp.sum(squares.reshape(tile_count, B, BLK_PX, B, BLK_PX), axis=(2, 4))  6.97 us
    integer_pow x1, other arithmetic, per_device(): squares = mask_tiles.astype(jnp.float32) ** 2  6.56 us
  transfers between devices with their start and end apart: 3, of which 3 were waited for; matrix products, arithmetic and copies ran while one was open for 4% of the time, Pallas kernels for 0%

commit v1 on v0

v1 whole, which is shorter than its diff:
```python
import functools

import jax
import jax.numpy as jnp
import ml_dtypes
import numpy as np
from jax import lax
from jax.experimental import pallas as pl
from jax.experimental.pallas import tpu as pltpu
from jax.sharding import PartitionSpec as P

BLK_PX = 64
CAP = 2
SC = 32
SR_DEV = 4
Q = 128
B = 8
REACH = 64
GAIN_SCALE = 50.0
LANES = 128
MESH = pl.DeviceIdType.MESH
F32 = jnp.float32
BF16 = jnp.bfloat16


def trig(freq_count, length):
    frequency = np.arange(freq_count) - freq_count // 2
    phases = np.mod(frequency[:, None] * np.arange(length)[None, :], length) * (2.0 * np.pi / length)
    return np.cos(phases), np.sin(phases)


def as_bf16(table):
    return np.asarray(table, np.float32).astype(ml_dtypes.bfloat16)


def in_columns(table):
    return np.stack(np.split(table, table.shape[1] // LANES, axis=1))


def whole(ref):
    return jnp.concatenate([ref[i] for i in range(ref.shape[0])], axis=1)


def wave_tables(nf, pixels):
    c, s = trig(nf, pixels)
    across = np.concatenate([c, s], axis=0).T
    down = np.concatenate([c[0::2], c[1::2], s[0::2], s[1::2]], axis=0)
    return as_bf16(across), as_bf16(down)


def image_tables(nf):
    c, s = trig(nf, Q)
    zero = np.zeros_like(c)
    right = np.block([[c, s, zero, zero], [zero, zero, c, s], [-s, c, zero, zero], [zero, zero, -s, c]])
    full = np.block([[c, s], [-s, c]]).T
    order = np.concatenate([np.arange(0, nf, 2), nf + np.arange(0, nf, 2), np.arange(1, nf, 2), nf + np.arange(1, nf, 2)])
    return as_bf16(right), as_bf16(full[:, order])


def resist_table(pixels):
    cp, sp = trig(Q, pixels)
    cq, sq = trig(Q, Q)
    frequency = np.arange(Q) - Q // 2
    weight = np.exp(-0.5 * (frequency * (4.0 / Q)) ** 2)[:, None]
    return as_bf16(((cp * weight).T @ cq + (sp * weight).T @ sq) / Q)


def spread_table(extent):
    places = np.arange(extent)
    weight = np.exp(-np.abs(places[:, None] - places[None, :]) / REACH)
    return weight / weight.sum(axis=1, keepdims=True)


def height_tables(strips):
    down = spread_table(strips * B).reshape(strips, B, strips * B).mean(axis=1).T
    down = np.pad(down, ((0, 0), (0, LANES - strips)))
    along = spread_table(SC * B).reshape(SC * B, SC, B).mean(axis=2).reshape(SC, B * SC)
    return down.astype(np.float32), along.astype(np.float32)


def imaging_kernel(
    n_tile, n_focus, strips, ker, nf,
    mask_hbm, class_ref, cell_ref, center_ref, w_ref, wave_x, wave_y, right_ref, left_ref, down_ref, along_ref,
    ret_ref,
    mask_v, sq_v, sp_v, out_v, in_v, hs_v, hr_v, zs_v, zr_v, shift_v, lit_v,
    mask_sem, h_send, h_recv, z_send, z_recv, s_send, s_recv, r_send, r_recv, own_sem,
):
    my_t, my_f = lax.axis_index("tile"), lax.axis_index("focus")
    tiles, px, _ = mask_v.shape
    half = nf // 2

    def ahead(o):
        return lax.rem(my_f + o, n_focus)

    def behind(o):
        return lax.rem(my_f + n_focus - o, n_focus)

    def above(o):
        return lax.rem(my_t + o, n_tile)

    def mask_copy(t):
        return pltpu.make_async_copy(mask_hbm.at[t], mask_v.at[t], mask_sem.at[t])

    for t in range(tiles):
        mask_copy(t).start()
    barrier = pltpu.get_barrier_semaphore()
    for o in range(1, n_focus):
        pl.semaphore_signal(barrier, inc=1, device_id=(my_t, ahead(o)), device_id_type=MESH)
    for o in range(1, n_tile):
        pl.semaphore_signal(barrier, inc=1, device_id=(above(o), my_f), device_id_type=MESH)

    def forward(t, carry):
        mask_copy(t).wait()
        mask = mask_v[t]
        wide = mask.astype(F32)
        sq_v[pl.ds(pl.multiple_of(t * B, B), B), :] = jnp.sum((wide * wide).reshape(B, BLK_PX, px), axis=1)
        projected = jnp.dot(mask, wave_x[...], preferred_element_type=F32).astype(BF16)
        raw = jnp.dot(whole(wave_y), projected, preferred_element_type=F32)
        top, bottom = raw[:nf], pltpu.roll(raw[nf:], nf, 1)
        real, imag = (top - bottom) / px, -(top + bottom) / px
        low = lax.broadcasted_iota(jnp.int32, (half, 2 * nf), 1) < nf
        packed_re = jnp.where(low, real[:half], pltpu.roll(real[half:], nf, 1))
        packed_im = jnp.where(low, pltpu.roll(imag[:half], nf, 1), imag[half:])
        sp_v[t] = jnp.concatenate([packed_re, packed_im], axis=0).astype(BF16)
        return carry

    lax.fori_loop(0, tiles, forward, 0)

    sums = sq_v[...]
    high = sums.astype(BF16)
    rest = (sums - high.astype(F32)).astype(BF16)
    spot = lax.broadcasted_iota(jnp.int32, (px, B * SC), 0) // BLK_PX
    group = lax.broadcasted_iota(jnp.int32, (px, B * SC), 1) // SC
    fold = jnp.where(spot == group, 1.0 / (BLK_PX * BLK_PX), 0.0).astype(BF16)
    both = jnp.dot(jnp.concatenate([high, rest], axis=0), fold, preferred_element_type=F32)
    density = both[: tiles * B] + both[tiles * B :]
    row_of = lax.broadcasted_iota(jnp.int32, (tiles * B, LANES), 0)
    lane_of = lax.broadcasted_iota(jnp.int32, (tiles * B, LANES), 1)
    cell_rows = jnp.zeros((tiles * B, LANES), jnp.int32)
    classes, cells, slots = [], [], []
    for t in range(tiles):
        classes.append(class_ref[t])
        cells.append(cell_ref[t])
        rank = jnp.int32(0)
        for before in range(t):
            rank = rank + jnp.where(classes[before] == classes[t], 1, 0)
        slots.append(classes[t] * CAP + rank)
        cell_rows = jnp.where(row_of // B == t, cells[t], cell_rows)
    strip_rows = cell_rows // SC
    wanted_column = jnp.where(lane_of == cell_rows - strip_rows * SC, 1.0, 0.0)[:, :SC]
    wanted_row = jnp.concatenate(
        [jnp.where(lane_of + first == strip_rows * B + row_of % B, 1.0, 0.0) for first in range(0, strips * B, LANES)],
        axis=1)
    exact = dict(precision=lax.Precision.HIGHEST, preferred_element_type=F32)
    downs = jnp.dot(wanted_row, down_ref[...], **exact)
    alongs = jnp.dot(wanted_column, along_ref[...], **exact)
    share = lax.dot_general(downs, density * alongs, (((0,), (0,)), ((), ())), **exact)[:strips]
    share = share[:, :LANES] + share[:, LANES:]
    share = share + pltpu.roll(share, 2 * SC, 1)
    share = share + pltpu.roll(share, SC, 1)
    row_at = lax.broadcasted_iota(jnp.int32, (tiles, LANES), 0)
    lane_at = lax.broadcasted_iota(jnp.int32, (tiles, LANES), 1)
    info = jnp.zeros((tiles, LANES), F32)
    for t in range(tiles):
        entry = jnp.where(lane_at == 0, cells[t], slots[t]).astype(F32)
        info = jnp.where(row_at == t, entry, info)
    hs_v[:strips] = share
    hs_v[strips:] = info
    hr_v[0] = hs_v[...]

    pl.semaphore_wait(barrier, n_focus - 1 + n_tile - 1)

    def h_copy(o):
        return pltpu.make_async_remote_copy(
            src_ref=hs_v, dst_ref=hr_v.at[o], send_sem=h_send.at[o], recv_sem=h_recv.at[o],
            device_id=(my_t, ahead(o)), device_id_type=MESH)

    def z_copy(o):
        return pltpu.make_async_remote_copy(
            src_ref=zs_v, dst_ref=zr_v.at[o], send_sem=z_send.at[o], recv_sem=z_recv.at[o],
            device_id=(above(o), my_f), device_id_type=MESH)

    def s_copy(o):
        return pltpu.make_async_remote_copy(
            src_ref=out_v.at[o], dst_ref=in_v.at[o], send_sem=s_send.at[o], recv_sem=s_recv.at[o],
            device_id=(my_t, ahead(o)), device_id_type=MESH)

    def r_copy(o):
        return pltpu.make_async_remote_copy(
            src_ref=lit_v.at[o], dst_ref=ret_ref.at[my_f], send_sem=r_send.at[o], recv_sem=r_recv.at[o],
            device_id=(my_t, behind(o)), device_id_type=MESH)

    for o in range(1, n_focus):
        h_copy(o).start()

    slot_tiles = [jnp.full((8, LANES), slots[t], jnp.int32) for t in range(tiles)]
    for o in range(n_focus):
        target = in_v if o == 0 else out_v
        for j in range(CAP):
            name = ahead(o) * CAP + j
            chosen = jnp.zeros((2 * nf // 16, 8, 2 * nf), F32)
            for t in range(tiles):
                chosen = jnp.where((slot_tiles[t] == name)[None], sp_v[t].astype(F32).reshape(chosen.shape), chosen)
            target[o, j] = chosen.reshape(nf, 2 * nf).astype(BF16)
        if o > 0:
            s_copy(o).start()

    for o in range(1, n_focus):
        h_copy(o).wait_recv()
    subtotal = hr_v[0, :strips]
    for o in range(1, n_focus):
        subtotal = subtotal + hr_v[o, :strips]
    zs_v[...] = subtotal
    for o in range(1, n_tile):
        z_copy(o).start()
    for o in range(1, n_tile):
        z_copy(o).wait_recv()
    heights = subtotal
    for o in range(1, n_tile):
        heights = heights + zr_v[o]
    average = jnp.sum(heights, keepdims=True) / (strips * LANES)
    names = hr_v[:, strips:, :].reshape(n_focus * tiles, LANES)
    cell_col, slot_col = names[:, 0:1], names[:, 1:2]
    strip_col = jnp.floor(cell_col / SC)
    column_col = cell_col - strip_col * SC
    picked = jnp.zeros((n_focus * tiles, LANES), F32)
    for r in range(strips):
        picked = jnp.where(strip_col == r, heights[r : r + 1], picked)
    lane = lax.broadcasted_iota(jnp.int32, picked.shape, 1).astype(F32)
    own = jnp.sum(jnp.where(lane == column_col, picked, 0.0), axis=1, keepdims=True)
    defocus = GAIN_SCALE * (own - average) - center_ref[my_f]
    for j in range(CAP):
        here = slot_col == (my_f * CAP + j).astype(F32)
        kept = jnp.broadcast_to(jnp.where(here, defocus, 0.0), picked.shape)
        shift_v[j] = jnp.sum(kept.reshape(n_focus, tiles, LANES), axis=1)

    def image(o, j):
        d = shift_v[j, pl.ds(o, 1), :]
        spec = in_v[o, j].astype(F32)
        sr, si = spec[:half][None], spec[half:][None]
        w = [w_ref[:, i].astype(F32) for i in range(4)]
        kr, ki = w[0] + d[None] * w[2], w[1] + d[None] * w[3]
        pr = (kr * sr - ki * si).astype(BF16).reshape(ker * half, 2 * nf)
        pi = (kr * si + ki * sr).astype(BF16).reshape(ker * half, 2 * nf)
        across = jnp.dot(jnp.concatenate([pr, pi], axis=1), whole(right_ref), preferred_element_type=F32).astype(BF16)
        left = left_ref[...]
        total = jnp.zeros((Q, Q), F32)
        for k in range(0, ker, 2):
            sides = []
            for m in (k, k + 1):
                rows = across[m * half : (m + 1) * half]
                sides.append(jnp.concatenate([rows[:, i * Q : (i + 1) * Q] for i in range(4)], axis=0))
            fields = jnp.dot(left, jnp.concatenate(sides, axis=1), preferred_element_type=F32)
            power = fields * fields
            total = total + ((power[:Q, :Q] + power[Q:, :Q]) + (power[:Q, Q:] + power[Q:, Q:]))
        return (total / ker).astype(BF16)

    own_copy = pltpu.make_async_copy(lit_v.at[0], ret_ref.at[my_f], own_sem)
    for j in range(CAP):
        lit_v[0, j] = image(0, j)
    own_copy.start()

    def serve(o, carry):
        s_copy(o).wait_recv()
        for j in range(CAP):
            lit_v[o, j] = image(o, j)
        r_copy(o).start()
        return carry

    lax.fori_loop(1, n_focus, serve, 0)
    own_copy.wait()
    for o in range(1, n_focus):
        r_copy(o).wait_recv()
    for o in range(1, n_focus):
        h_copy(o).wait_send()
        s_copy(o).wait_send()
        r_copy(o).wait_send()
    for o in range(1, n_tile):
        z_copy(o).wait_send()


def resist_kernel(per, class_ref, lit_ref, wide_ref, tall_ref, out_ref):
    first = pl.program_id(0) * per
    for i in range(per):
        t = first + i
        own = class_ref[t]
        rank = lax.fori_loop(0, t, lambda b, r: r + jnp.where(class_ref[b] == own, 1, 0), jnp.int32(0))
        light = lit_ref[own * CAP + rank]
        half_way = jnp.dot(light, whole(wide_ref), preferred_element_type=F32).astype(BF16)
        out_ref[i] = jnp.dot(tall_ref[...], half_way, preferred_element_type=F32).astype(BF16)


def per_device(n_tile, n_focus, mask_tiles, class_of_tile, cell_of_tile, kernels, class_center):
    tiles, px, _ = mask_tiles.shape
    _, ker, parts, area = kernels.shape
    nf = int(round(area ** 0.5))
    half = nf // 2
    strips = SR_DEV * n_tile
    wave_x, wave_y = wave_tables(nf, px)
    right, left = image_tables(nf)
    down, along = height_tables(strips)
    resist = resist_table(px)
    weights = kernels.reshape(ker, parts, half, 2 * nf)
    classes = class_of_tile.reshape(tiles)
    smem = pl.BlockSpec(memory_space=pltpu.SMEM)
    vmem = pl.BlockSpec(memory_space=pltpu.VMEM)
    anywhere = pl.BlockSpec(memory_space=pl.ANY)
    dma = pltpu.SemaphoreType.DMA
    slots = n_focus * CAP
    row_work = slots * ker * (half * 4 * nf * 4 * Q + 2 * Q * 2 * nf * Q)
    returned = pl.pallas_call(
        functools.partial(imaging_kernel, n_tile, n_focus, strips, ker, nf),
        out_shape=jax.ShapeDtypeStruct((n_focus, CAP, Q, Q), BF16),
        in_specs=[anywhere, smem, smem, smem] + [vmem] * 7,
        out_specs=anywhere,
        scratch_shapes=[
            pltpu.VMEM((tiles, px, px), BF16),
            pltpu.VMEM((tiles * B, px), F32),
            pltpu.VMEM((tiles, nf, 2 * nf), BF16),
            pltpu.VMEM((n_focus, CAP, nf, 2 * nf), BF16),
            pltpu.VMEM((n_focus, CAP, nf, 2 * nf), BF16),
            pltpu.VMEM((strips + tiles, LANES), F32),
            pltpu.VMEM((n_focus, strips + tiles, LANES), F32),
            pltpu.VMEM((strips, LANES), F32),
            pltpu.VMEM((n_tile, strips, LANES), F32),
            pltpu.VMEM((CAP, n_focus, LANES), F32),
            pltpu.VMEM((n_focus, CAP, Q, Q), BF16),
            dma((tiles,)),
            dma((n_focus,)), dma((n_focus,)),
            dma((n_tile,)), dma((n_tile,)),
            dma((n_focus,)), dma((n_focus,)),
            dma((n_focus,)), dma((n_focus,)),
            dma,
        ],
        compiler_params=pltpu.CompilerParams(
            collective_id=0, has_side_effects=True, vmem_limit_bytes=56 * 1024 * 1024),
        cost_estimate=pl.CostEstimate(flops=2 * row_work, bytes_accessed=8 * 1024 * 1024, transcendentals=0),
        name="imaging",
    )(mask_tiles, classes, cell_of_tile, class_center, weights, wave_x, in_columns(wave_y), in_columns(right), left, down, along)
    per = 2 if tiles % 2 == 0 else 1
    return pl.pallas_call(
        functools.partial(resist_kernel, per),
        out_shape=jax.ShapeDtypeStruct((tiles, px, px), BF16),
        grid=(tiles // per,),
        in_specs=[smem, vmem, vmem, vmem],
        out_specs=pl.BlockSpec((per, px, px), lambda i: (i, 0, 0)),
        compiler_params=pltpu.CompilerParams(vmem_limit_bytes=48 * 1024 * 1024),
        cost_estimate=pl.CostEstimate(
            flops=2 * tiles * Q * px * (Q + px), bytes_accessed=2 * tiles * px * px, transcendentals=0),
        name="resist",
    )(classes, returned.reshape(slots, Q, Q), in_columns(resist.T), resist)


def solution(mesh):
    placed = (
        P(("tile", "focus"), None, None),
        P(("tile", "focus"), None),
        P(("tile", "focus")),
        P("focus", None, None, None),
        P(),
    )
    return jax.shard_map(
        functools.partial(per_device, mesh.shape["tile"], mesh.shape["focus"]),
        mesh=mesh,
        in_specs=placed,
        out_specs=P(("tile", "focus"), None, None),
        check_vma=False,
    )
```

time: 281 us -> 44 us (0.16)
  waiting for transfers between devices: 129 us -> 0 us
  local copies, waits for them, and re-layouts: 58.8 us -> 3.84 us
  Pallas kernels: 0 us -> 39.9 us
  matrix products: 33.1 us -> 0 us
  other arithmetic: 28.3 us -> 0 us
  between operations: 14.3 us -> 0.04 us
  blocking collectives: 8.08 us -> 0 us
  starting transfers between devices: 7.31 us -> 0 us
    psum x1 -> x0, waiting for transfers between devices: 117 us -> none  [per_device(): totals = lax.psum(partial_value, ('tile', 'focus'))]
    pallas_call x0 -> x2, Pallas kernels: none -> 39.9 us  [the longest x1 34.6 us: per_device(): pl.pallas_call(functools.partial(imaging_kernel, n_tile, n_focus, strips,...]
    dot_general x25 -> x0, matrix products: 33.1 us -> none  [the longest x4 7.37 us: image_one(): jnp.einsum('pu,kuv->pkv', left_table[:, NF:], across[:, :, Q:], preferred...]
    mul x20 -> x0, local copies, waits for them, and re-layouts: 16.3 us -> none  [the longest x8 6.24 us: image_one(): prod_re = kern_re * spec_parts[0] - kern_im * spec_parts[1]]
    reshape x8 -> x1, local copies, waits for them, and re-layouts: 18 us -> 2.8 us  [per_device(): weights = kernels.reshape(ker, parts, half, 2 * nf)]
    another operation x9 -> x0, other arithmetic: 11.8 us -> none
    all_to_all x2 -> x0, waiting for transfers between devices: 11.3 us -> none  [the longest x1 5.88 us: per_device(): lax.all_to_all(for_sending(lit_slots.reshape(sources, slots_each, Q * Q))...]
    convert_element_type x4 -> x0, local copies, waits for them, and re-layouts: 9.02 us -> none  [the longest x1 6.44 us: per_device(): return jnp.einsum('xq,tqy->txy', resist_rows, half_way, preferred_element...]
  transfers between devices with their start and end apart: 3 -> 0, of which waited for: 3 -> 0; matrix products, arithmetic and copies ran while one was open for 4% -> 0% of each run, Pallas kernels for 0% -> 0%
where the time goes in v1:
time: 44 us; the launch traced here: 43.8 us
  Pallas kernels  39.9 us (91%)
  local copies, waits for them, and re-layouts  3.84 us (9%)
    pallas_call x1, Pallas kernels, per_device(): pl.pallas_call(functools.partial(imaging_kernel, n_tile, n_focus, strips,...  34.6 us
    pallas_call x1, Pallas kernels, per_device(): pl.pallas_call(functools.partial(resist_kernel, per), out_shape=jax.Shape...  5.29 us
    reshape x1, local copies, waits for them, and re-layouts, per_device(): weights = kernels.reshape(ker, parts, half, 2 * nf)  2.8 us
    unnamed x8, local copies, waits for them, and re-layouts  1.05 us

profile of v1, /device:TPU:0, one launch (start us, length us, event | category | flops | bytes accessed | tf_op | source)
XLA Modules:
  0.0 43.8 jit_solution(16624029435387846451)
XLA Ops:
  0.0 2.8 %reshape.10.w_ref = bf16[24,4,32,128]{3,2,1,0:T(8,128)(2,1)} reshape(bf16[1,24,4,4096]{3,2,1,0:T(4,128)(2,1)} %param.16) | data formatting | bytes 1572864 | tf_op jit(solution)/shard_map/reshape | solution.py:303
  2.8 0.0 copy-start.1
  2.8 0.0 copy-start.2
  2.8 0.0 copy-start.3
  2.8 34.6 %imaging.1 = bf16[8,2,128,128]{3,2,1,0:T(8,128)(2,1)} custom-call(bf16[8,512,512]{2,1,0:T(8,128)(2,1)} %mask_hbm.1, s32[8]{0:T(128)} %bitcast.3, s32[8]{0:T(128)} %cell_ref.1, f32[8]{0:T(128)} %center_ref.1, bf16[24,4,32,128]{3,2,1,0:T(8,128)(2,1)} %reshape.10.w_ref, bf16[512,128]{1,0:T(8,128)(2,1)} %constant.16.clone.wave_x, ...), custom_call_target="tpu_custom_call" | custom-call | flops 6442450944 | bytes 8388608 | tf_op jit(solution)/shard_map/imaging/pallas_call | solution.py:311
  37.4 0.0 copy-done.1
  37.5 0.0 copy-done.2
  37.5 0.0 copy-done.3
  37.5 0.0 copy-start
  37.5 1.0 %copy-done = bf16[8,2,128,128]{3,2,1,0:T(8,128)(2,1)S(1)} copy-done((bf16[8,2,128,128]{3,2,1,0:T(8,128)(2,1)S(1)}, bf16[8,2,128,128]{3,2,1,0:T(8,128)(2,1)}, u32[]{:S(2)}) %copy-start) | copy-done | bytes 524312
  38.5 5.3 %resist.1 = bf16[8,512,512]{2,1,0:T(8,128)(2,1)} custom-call(s32[8]{0:T(128)S(1)} %bitcast.4, bf16[16,128,128]{2,1,0:T(8,128)(2,1)S(1)} %bitcast.2, bf16[4,128,128]{2,1,0:T(8,128)(2,1)S(1)} %copy-done.2, bf16[512,128]{1,0:T(8,128)(2,1)S(1)} %copy-done.1), custom_call_target="tpu_custom_call" | custom-call | flops 671088640 | bytes 4194304 | tf_op jit(solution)/shard_map/resist/pallas_call | solution.py:341
Async XLA Ops:
  2.8 34.6 %copy-start.1 = (bf16[512,128]{1,0:T(8,128)(2,1)S(1)}, bf16[512,128]{1,0:T(8,128)(2,1)}, u32[]{:S(2)}) copy-start(bf16[512,128]{1,0:T(8,128)(2,1)} %constant.23.clone.tall_ref) | copy-start | bytes 393220
  2.8 34.7 %copy-start.2 = (bf16[4,128,128]{2,1,0:T(8,128)(2,1)S(1)}, bf16[4,128,128]{2,1,0:T(8,128)(2,1)}, u32[]{:S(2)}) copy-start(bf16[4,128,128]{2,1,0:T(8,128)(2,1)} %constant.22.clone.wide_ref) | copy-start | bytes 393220
  2.8 34.7 %copy-start.3 = (s32[8,1]{0,1:T(1,128)S(1)}, s32[8,1]{0,1:T(1,128)}, u32[]{:S(2)}) copy-start(s32[8,1]{0,1:T(1,128)} %param.14) | copy-start | bytes 100
  37.5 1.0 %copy-start = (bf16[8,2,128,128]{3,2,1,0:T(8,128)(2,1)S(1)}, bf16[8,2,128,128]{3,2,1,0:T(8,128)(2,1)}, u32[]{:S(2)}) copy-start(bf16[8,2,128,128]{3,2,1,0:T(8,128)(2,1)} %imaging.1) | copy-start | bytes 1572868

commit v2 on v1

--- a/solution.py
+++ b/solution.py
@@ -80,10 +80,11 @@
 
 def imaging_kernel(
     n_tile, n_focus, strips, ker, nf,
-    mask_hbm, class_ref, cell_ref, center_ref, w_ref, wave_x, wave_y, right_ref, left_ref, down_ref, along_ref,
+    mask_hbm, class_ref, cell_ref, center_ref, w_hbm, wave_x_hbm, wave_y_hbm, right_hbm, left_hbm, down_hbm, along_hbm,
     ret_ref,
-    mask_v, sq_v, sp_v, out_v, in_v, hs_v, hr_v, zs_v, zr_v, shift_v, lit_v,
-    mask_sem, h_send, h_recv, z_send, z_recv, s_send, s_recv, r_send, r_recv, own_sem,
+    mask_v, sq_v, sp_v, out_v, in_v, hs_v, hr_v, zs_v, zr_v, shift_v, lit_v, raw_v, w_v, fil_v,
+    wave_x, wave_y, right_ref, left_ref, down_ref, along_ref,
+    mask_sem, h_send, h_recv, z_send, z_recv, s_send, s_recv, r_send, r_recv, own_sem, table_sem,
 ):
     my_t, my_f = lax.axis_index("tile"), lax.axis_index("focus")
     tiles, px, _ = mask_v.shape
@@ -101,20 +102,33 @@
     def mask_copy(t):
         return pltpu.make_async_copy(mask_hbm.at[t], mask_v.at[t], mask_sem.at[t])
 
+    fetched = [
+        (down_hbm, down_ref), (along_hbm, along_ref), (wave_x_hbm, wave_x), (wave_y_hbm, wave_y),
+        (w_hbm.at[0], raw_v), (right_hbm, right_ref), (left_hbm, left_ref)]
+    tables = [pltpu.make_async_copy(src, dst, table_sem.at[i]) for i, (src, dst) in enumerate(fetched)]
+
     for t in range(tiles):
         mask_copy(t).start()
+    for table in tables:
+        table.start()
     barrier = pltpu.get_barrier_semaphore()
     for o in range(1, n_focus):
         pl.semaphore_signal(barrier, inc=1, device_id=(my_t, ahead(o)), device_id_type=MESH)
     for o in range(1, n_tile):
         pl.semaphore_signal(barrier, inc=1, device_id=(above(o), my_f), device_id_type=MESH)
 
-    def forward(t, carry):
+    def squares(t, carry):
         mask_copy(t).wait()
-        mask = mask_v[t]
-        wide = mask.astype(F32)
+        wide = mask_v[t].astype(F32)
         sq_v[pl.ds(pl.multiple_of(t * B, B), B), :] = jnp.sum((wide * wide).reshape(B, BLK_PX, px), axis=1)
-        projected = jnp.dot(mask, wave_x[...], preferred_element_type=F32).astype(BF16)
+        return carry
+
+    lax.fori_loop(0, tiles, squares, 0)
+    tables[0].wait()
+    tables[1].wait()
+
+    def spectrum(t):
+        projected = jnp.dot(mask_v[t], wave_x[...], preferred_element_type=F32).astype(BF16)
         raw = jnp.dot(whole(wave_y), projected, preferred_element_type=F32)
         top, bottom = raw[:nf], pltpu.roll(raw[nf:], nf, 1)
         real, imag = (top - bottom) / px, -(top + bottom) / px
@@ -122,9 +136,11 @@
         packed_re = jnp.where(low, real[:half], pltpu.roll(real[half:], nf, 1))
         packed_im = jnp.where(low, pltpu.roll(imag[:half], nf, 1), imag[half:])
         sp_v[t] = jnp.concatenate([packed_re, packed_im], axis=0).astype(BF16)
+
+    def forward(step, carry):
+        for i in range(2):
+            spectrum(2 * step + i)
         return carry
-
-    lax.fori_loop(0, tiles, forward, 0)
 
     sums = sq_v[...]
     high = sums.astype(BF16)
@@ -193,6 +209,18 @@
     for o in range(1, n_focus):
         h_copy(o).start()
 
+    tables[2].wait()
+    tables[3].wait()
+    lax.fori_loop(0, tiles // 2, forward, 0)
+
+    for o in range(1, n_focus):
+        h_copy(o).wait_recv()
+    subtotal = hr_v[0, :strips]
+    for o in range(1, n_focus):
+        subtotal = subtotal + hr_v[o, :strips]
+    zs_v[...] = subtotal
+    for o in range(1, n_tile):
+        z_copy(o).start()
     slot_tiles = [jnp.full((8, LANES), slots[t], jnp.int32) for t in range(tiles)]
     for o in range(n_focus):
         target = in_v if o == 0 else out_v
@@ -205,14 +233,14 @@
         if o > 0:
             s_copy(o).start()
 
-    for o in range(1, n_focus):
-        h_copy(o).wait_recv()
-    subtotal = hr_v[0, :strips]
-    for o in range(1, n_focus):
-        subtotal = subtotal + hr_v[o, :strips]
-    zs_v[...] = subtotal
-    for o in range(1, n_tile):
-        z_copy(o).start()
+    tables[4].wait()
+
+    def lay(k, carry):
+        for b in range(half):
+            w_v[k, pl.ds(b, 4, stride=half), :] = raw_v[k, :, b * 2 * nf : (b + 1) * 2 * nf].astype(F32)
+        return carry
+
+    lax.fori_loop(0, ker, lay, 0)
     for o in range(1, n_tile):
         z_copy(o).wait_recv()
     heights = subtotal
@@ -234,18 +262,23 @@
         kept = jnp.broadcast_to(jnp.where(here, defocus, 0.0), picked.shape)
         shift_v[j] = jnp.sum(kept.reshape(n_focus, tiles, LANES), axis=1)
 
-    def image(o, j):
+    def filtered(o, j, m):
         d = shift_v[j, pl.ds(o, 1), :]
         spec = in_v[o, j].astype(F32)
-        sr, si = spec[:half][None], spec[half:][None]
-        w = [w_ref[:, i].astype(F32) for i in range(4)]
-        kr, ki = w[0] + d[None] * w[2], w[1] + d[None] * w[3]
-        pr = (kr * sr - ki * si).astype(BF16).reshape(ker * half, 2 * nf)
-        pi = (kr * si + ki * sr).astype(BF16).reshape(ker * half, 2 * nf)
-        across = jnp.dot(jnp.concatenate([pr, pi], axis=1), whole(right_ref), preferred_element_type=F32).astype(BF16)
+        sr, si = spec[:half], spec[half:]
+        rows = []
+        for k in (m, m + 1):
+            w = [w_v[k, i * half : (i + 1) * half, :] for i in range(4)]
+            kr, ki = w[0] + d * w[2], w[1] + d * w[3]
+            rows.append(jnp.concatenate([kr * sr - ki * si, kr * si + ki * sr], axis=1).astype(BF16))
+        return jnp.concatenate(rows, axis=0)
+
+    def image(now, after):
+        across = jnp.dot(fil_v[now], whole(right_ref), preferred_element_type=F32).astype(BF16)
         left = left_ref[...]
         total = jnp.zeros((Q, Q), F32)
         for k in range(0, ker, 2):
+            fil_v[1 - now, k * half : (k + 2) * half, :] = filtered(*after, k)
             sides = []
             for m in (k, k + 1):
                 rows = across[m * half : (m + 1) * half]
@@ -256,18 +289,30 @@
         return (total / ker).astype(BF16)
 
     own_copy = pltpu.make_async_copy(lit_v.at[0], ret_ref.at[my_f], own_sem)
-    for j in range(CAP):
-        lit_v[0, j] = image(0, j)
+    tables[5].wait()
+    tables[6].wait()
+    s_copy(1).wait_recv()
+    for k in range(0, ker, 2):
+        fil_v[0, k * half : (k + 2) * half, :] = filtered(1, 0, k)
+
+    def serve(step, carry):
+        o = lax.rem(step + 1, n_focus)
+        following = lax.rem(step + 2, n_focus)
+        for j in range(CAP):
+            if j == CAP - 1:
+                @pl.when(step < n_focus - 2)
+                def _():
+                    s_copy(following).wait_recv()
+            lit_v[o, j] = image(j % 2, (o, j + 1) if j < CAP - 1 else (following, 0))
+
+        @pl.when(o != 0)
+        def _():
+            r_copy(o).start()
+
+        return carry
+
+    lax.fori_loop(0, n_focus, serve, 0)
     own_copy.start()
-
-    def serve(o, carry):
-        s_copy(o).wait_recv()
-        for j in range(CAP):
-            lit_v[o, j] = image(o, j)
-        r_copy(o).start()
-        return carry
-
-    lax.fori_loop(1, n_focus, serve, 0)
     own_copy.wait()
     for o in range(1, n_focus):
         r_copy(o).wait_recv()
@@ -279,15 +324,29 @@
         z_copy(o).wait_send()
 
 
-def resist_kernel(per, class_ref, lit_ref, wide_ref, tall_ref, out_ref):
-    first = pl.program_id(0) * per
-    for i in range(per):
-        t = first + i
+def resist_kernel(class_ref, lit_hbm, wide_ref, tall_ref, out_ref, lit_v, out_v, in_sem, out_sem):
+    tiles = out_v.shape[0]
+
+    def fetch(t):
         own = class_ref[t]
-        rank = lax.fori_loop(0, t, lambda b, r: r + jnp.where(class_ref[b] == own, 1, 0), jnp.int32(0))
-        light = lit_ref[own * CAP + rank]
-        half_way = jnp.dot(light, whole(wide_ref), preferred_element_type=F32).astype(BF16)
-        out_ref[i] = jnp.dot(tall_ref[...], half_way, preferred_element_type=F32).astype(BF16)
+        rank = jnp.int32(0)
+        for b in range(t):
+            rank = rank + jnp.where(class_ref[b] == own, 1, 0)
+        return pltpu.make_async_copy(lit_hbm.at[own * CAP + rank], lit_v.at[t], in_sem.at[t])
+
+    def leave(t):
+        return pltpu.make_async_copy(out_v.at[t], out_ref.at[t], out_sem.at[t])
+
+    copies = [fetch(t) for t in range(tiles)]
+    for copy in copies:
+        copy.start()
+    for t in range(tiles):
+        copies[t].wait()
+        half_way = jnp.dot(lit_v[t], whole(wide_ref), preferred_element_type=F32).astype(BF16)
+        out_v[t] = jnp.dot(tall_ref[...], half_way, preferred_element_type=F32).astype(BF16)
+        leave(t).start()
+    for t in range(tiles):
+        leave(t).wait()
 
 
 def per_device(n_tile, n_focus, mask_tiles, class_of_tile, cell_of_tile, kernels, class_center):
@@ -300,7 +359,7 @@
     right, left = image_tables(nf)
     down, along = height_tables(strips)
     resist = resist_table(px)
-    weights = kernels.reshape(ker, parts, half, 2 * nf)
+    tables = [wave_x, in_columns(wave_y), in_columns(right), left, down, along]
     classes = class_of_tile.reshape(tiles)
     smem = pl.BlockSpec(memory_space=pltpu.SMEM)
     vmem = pl.BlockSpec(memory_space=pltpu.VMEM)
@@ -311,7 +370,7 @@
     returned = pl.pallas_call(
         functools.partial(imaging_kernel, n_tile, n_focus, strips, ker, nf),
         out_shape=jax.ShapeDtypeStruct((n_focus, CAP, Q, Q), BF16),
-        in_specs=[anywhere, smem, smem, smem] + [vmem] * 7,
+        in_specs=[anywhere, smem, smem, smem] + [anywhere] * 7,
         out_specs=anywhere,
         scratch_shapes=[
             pltpu.VMEM((tiles, px, px), BF16),
@@ -325,26 +384,31 @@
             pltpu.VMEM((n_tile, strips, LANES), F32),
             pltpu.VMEM((CAP, n_focus, LANES), F32),
             pltpu.VMEM((n_focus, CAP, Q, Q), BF16),
+            pltpu.VMEM((ker, parts, area), BF16),
+            pltpu.VMEM((ker, parts * half, 2 * nf), F32),
+            pltpu.VMEM((2, ker * half, 4 * nf), BF16),
+        ] + [pltpu.VMEM(table.shape, table.dtype) for table in tables] + [
             dma((tiles,)),
             dma((n_focus,)), dma((n_focus,)),
             dma((n_tile,)), dma((n_tile,)),
             dma((n_focus,)), dma((n_focus,)),
             dma((n_focus,)), dma((n_focus,)),
             dma,
+            dma((len(tables) + 1,)),
         ],
         compiler_params=pltpu.CompilerParams(
             collective_id=0, has_side_effects=True, vmem_limit_bytes=56 * 1024 * 1024),
         cost_estimate=pl.CostEstimate(flops=2 * row_work, bytes_accessed=8 * 1024 * 1024, transcendentals=0),
         name="imaging",
-    )(mask_tiles, classes, cell_of_tile, class_center, weights, wave_x, in_columns(wave_y), in_columns(right), left, down, along)
-    per = 2 if tiles % 2 == 0 else 1
+    )(mask_tiles, classes, cell_of_tile, class_center, kernels, *tables)
     return pl.pallas_call(
-        functools.partial(resist_kernel, per),
+        resist_kernel,
         out_shape=jax.ShapeDtypeStruct((tiles, px, px), BF16),
-        grid=(tiles // per,),
-        in_specs=[smem, vmem, vmem, vmem],
-        out_specs=pl.BlockSpec((per, px, px), lambda i: (i, 0, 0)),
-        compiler_params=pltpu.CompilerParams(vmem_limit_bytes=48 * 1024 * 1024),
+        in_specs=[smem, anywhere, vmem, vmem],
+        out_specs=anywhere,
+        scratch_shapes=[
+            pltpu.VMEM((tiles, Q, Q), BF16), pltpu.VMEM((tiles, px, px), BF16), dma((tiles,)), dma((tiles,))],
+        compiler_params=pltpu.CompilerParams(vmem_limit_bytes=56 * 1024 * 1024),
         cost_estimate=pl.CostEstimate(
             flops=2 * tiles * Q * px * (Q + px), bytes_accessed=2 * tiles * px * px, transcendentals=0),
         name="resist",

time: 44 us -> 39.1 us (0.89)
  local copies, waits for them, and re-layouts: 3.84 us -> 0 us
  Pallas kernels: 39.9 us -> 38.9 us
    reshape x1 -> x0, local copies, waits for them, and re-layouts: 2.8 us -> none  [per_device(): weights = kernels.reshape(ker, parts, half, 2 * nf)]
    pallas_call x1, Pallas kernels: 34.6 us -> 32.7 us  [per_device(): pl.pallas_call(functools.partial(imaging_kernel, n_tile, n_focus, strips,...]
    unnamed x8 -> x0, local copies, waits for them, and re-layouts: 1.05 us -> none
    pallas_call x1, Pallas kernels: 5.29 us -> 6.18 us  [per_device(): pl.pallas_call(resist_kernel, out_shape=jax.ShapeDtypeStruct((tiles, px,...]
where the time goes in v2:
time: 39.1 us; the launch traced here: 38.9 us
  Pallas kernels  38.9 us (99%)
    pallas_call x1, Pallas kernels, per_device(): pl.pallas_call(functools.partial(imaging_kernel, n_tile, n_focus, strips,...  32.7 us
    pallas_call x1, Pallas kernels, per_device(): pl.pallas_call(resist_kernel, out_shape=jax.ShapeDtypeStruct((tiles, px,...  6.18 us

profile of v2, /device:TPU:0, one launch (start us, length us, event | category | flops | bytes accessed | tf_op | source)
XLA Modules:
  0.0 38.9 jit_solution(13535064976843610258)
XLA Ops:
  0.0 32.7 %imaging.1 = bf16[8,2,128,128]{3,2,1,0:T(8,128)(2,1)} custom-call(bf16[8,512,512]{2,1,0:T(8,128)(2,1)} %mask_hbm.1, s32[8]{0:T(128)} %bitcast.3, s32[8]{0:T(128)} %cell_ref.1, f32[8]{0:T(128)} %center_ref.1, bf16[1,24,4,4096]{3,2,1,0:T(4,128)(2,1)} %w_hbm.1, bf16[512,128]{1,0:T(8,128)(2,1)} %constant.16.clone.wave_x_hbm, ...), custom_call_target="tpu_custom_call" | custom-call | flops 6442450944 | bytes 8388608 | tf_op jit(solution)/shard_map/imaging/pallas_call | solution.py:370
  32.7 6.2 %resist.1 = bf16[8,512,512]{2,1,0:T(8,128)(2,1)} custom-call(s32[8]{0:T(128)} %bitcast.4, bf16[16,128,128]{2,1,0:T(8,128)(2,1)} %bitcast.2, bf16[4,128,128]{2,1,0:T(8,128)(2,1)} %constant.22.clone.wide_ref, bf16[512,128]{1,0:T(8,128)(2,1)} %constant.23.clone.tall_ref), custom_call_target="tpu_custom_call" | custom-call | flops 671088640 | bytes 4194304 | tf_op jit(solution)/shard_map/resist/pallas_call | solution.py:404

commit v3 on v2

--- a/solution.py
+++ b/solution.py
@@ -277,15 +277,17 @@
         across = jnp.dot(fil_v[now], whole(right_ref), preferred_element_type=F32).astype(BF16)
         left = left_ref[...]
         total = jnp.zeros((Q, Q), F32)
-        for k in range(0, ker, 2):
-            fil_v[1 - now, k * half : (k + 2) * half, :] = filtered(*after, k)
+        for first in range(0, ker, 4):
             sides = []
-            for m in (k, k + 1):
+            for m in range(first, min(first + 4, ker)):
+                if m % 2 == 0:
+                    fil_v[1 - now, m * half : (m + 2) * half, :] = filtered(*after, m)
                 rows = across[m * half : (m + 1) * half]
                 sides.append(jnp.concatenate([rows[:, i * Q : (i + 1) * Q] for i in range(4)], axis=0))
             fields = jnp.dot(left, jnp.concatenate(sides, axis=1), preferred_element_type=F32)
             power = fields * fields
-            total = total + ((power[:Q, :Q] + power[Q:, :Q]) + (power[:Q, Q:] + power[Q:, Q:]))
+            for i in range(len(sides)):
+                total = total + (power[:Q, i * Q : (i + 1) * Q] + power[Q:, i * Q : (i + 1) * Q])
         return (total / ker).astype(BF16)
 
     own_copy = pltpu.make_async_copy(lit_v.at[0], ret_ref.at[my_f], own_sem)
@@ -324,7 +326,7 @@
         z_copy(o).wait_send()
 
 
-def resist_kernel(class_ref, lit_hbm, wide_ref, tall_ref, out_ref, lit_v, out_v, in_sem, out_sem):
+def resist_kernel(class_ref, lit_hbm, wide_hbm, tall_hbm, out_ref, wide_ref, tall_ref, lit_v, out_v, sem, in_sem, out_sem):
     tiles = out_v.shape[0]
 
     def fetch(t):
@@ -337,13 +339,17 @@
     def leave(t):
         return pltpu.make_async_copy(out_v.at[t], out_ref.at[t], out_sem.at[t])
 
-    copies = [fetch(t) for t in range(tiles)]
+    wide_copy = pltpu.make_async_copy(wide_hbm, wide_ref, sem.at[0])
+    tall_copy = pltpu.make_async_copy(tall_hbm, tall_ref, sem.at[1])
+    copies = [wide_copy] + [fetch(t) for t in range(tiles)] + [tall_copy]
     for copy in copies:
         copy.start()
+    for copy in copies:
+        copy.wait()
+    wide, tall = whole(wide_ref), tall_ref[...]
+    half_way = jnp.dot(lit_v[...].reshape(tiles * Q, Q), wide, preferred_element_type=F32).astype(BF16)
     for t in range(tiles):
-        copies[t].wait()
-        half_way = jnp.dot(lit_v[t], whole(wide_ref), preferred_element_type=F32).astype(BF16)
-        out_v[t] = jnp.dot(tall_ref[...], half_way, preferred_element_type=F32).astype(BF16)
+        out_v[t] = jnp.dot(tall, half_way[t * Q : (t + 1) * Q], preferred_element_type=F32).astype(BF16)
         leave(t).start()
     for t in range(tiles):
         leave(t).wait()
@@ -359,10 +365,10 @@
     right, left = image_tables(nf)
     down, along = height_tables(strips)
     resist = resist_table(px)
+    wide = in_columns(resist.T)
     tables = [wave_x, in_columns(wave_y), in_columns(right), left, down, along]
     classes = class_of_tile.reshape(tiles)
     smem = pl.BlockSpec(memory_space=pltpu.SMEM)
-    vmem = pl.BlockSpec(memory_space=pltpu.VMEM)
     anywhere = pl.BlockSpec(memory_space=pl.ANY)
     dma = pltpu.SemaphoreType.DMA
     slots = n_focus * CAP
@@ -404,15 +410,17 @@
     return pl.pallas_call(
         resist_kernel,
         out_shape=jax.ShapeDtypeStruct((tiles, px, px), BF16),
-        in_specs=[smem, anywhere, vmem, vmem],
+        in_specs=[smem, anywhere, anywhere, anywhere],
         out_specs=anywhere,
         scratch_shapes=[
-            pltpu.VMEM((tiles, Q, Q), BF16), pltpu.VMEM((tiles, px, px), BF16), dma((tiles,)), dma((tiles,))],
+            pltpu.VMEM(wide.shape, BF16), pltpu.VMEM(resist.shape, BF16),
+            pltpu.VMEM((tiles, Q, Q), BF16), pltpu.VMEM((tiles, px, px), BF16),
+            dma((2,)), dma((tiles,)), dma((tiles,))],
         compiler_params=pltpu.CompilerParams(vmem_limit_bytes=56 * 1024 * 1024),
         cost_estimate=pl.CostEstimate(
             flops=2 * tiles * Q * px * (Q + px), bytes_accessed=2 * tiles * px * px, transcendentals=0),
         name="resist",
-    )(classes, returned.reshape(slots, Q, Q), in_columns(resist.T), resist)
+    )(classes, returned.reshape(slots, Q, Q), wide, resist)
 
 
 def solution(mesh):

time: 39.1 us -> 37.3 us (0.954)
  Pallas kernels: 38.9 us -> 37.2 us
    pallas_call x1, Pallas kernels: 6.18 us -> 4.5 us  [per_device(): pl.pallas_call(resist_kernel, out_shape=jax.ShapeDtypeStruct((tiles, px,...]
where the time goes in v3:
time: 37.3 us; the launch traced here: 37.2 us
  Pallas kernels  37.2 us (100%)
    pallas_call x1, Pallas kernels, per_device(): pl.pallas_call(functools.partial(imaging_kernel, n_tile, n_focus, strips,...  32.7 us
    pallas_call x1, Pallas kernels, per_device(): pl.pallas_call(resist_kernel, out_shape=jax.ShapeDtypeStruct((tiles, px,...  4.5 us

profile of v3, /device:TPU:0, one launch (start us, length us, event | category | flops | bytes accessed | tf_op | source)
XLA Modules:
  0.0 37.2 jit_solution(11575817507210164632)
XLA Ops:
  0.0 32.7 %imaging.1 = bf16[8,2,128,128]{3,2,1,0:T(8,128)(2,1)} custom-call(bf16[8,512,512]{2,1,0:T(8,128)(2,1)} %mask_hbm.1, s32[8]{0:T(128)} %bitcast.3, s32[8]{0:T(128)} %cell_ref.1, f32[8]{0:T(128)} %center_ref.1, bf16[1,24,4,4096]{3,2,1,0:T(4,128)(2,1)} %w_hbm.1, bf16[512,128]{1,0:T(8,128)(2,1)} %constant.16.clone.wave_x_hbm, ...), custom_call_target="tpu_custom_call" | custom-call | flops 6442450944 | bytes 8388608 | tf_op jit(solution)/shard_map/imaging/pallas_call | solution.py:376
  32.7 4.5 %resist.1 = bf16[8,512,512]{2,1,0:T(8,128)(2,1)} custom-call(s32[8]{0:T(128)} %bitcast.4, bf16[16,128,128]{2,1,0:T(8,128)(2,1)} %bitcast.2, bf16[4,128,128]{2,1,0:T(8,128)(2,1)} %constant.22.clone.wide_hbm, bf16[512,128]{1,0:T(8,128)(2,1)} %constant.23.clone.tall_hbm), custom_call_target="tpu_custom_call" | custom-call | flops 671088640 | bytes 4194304 | tf_op jit(solution)/shard_map/resist/pallas_call | solution.py:410

commit v4 on v3

--- a/solution.py
+++ b/solution.py
@@ -82,7 +82,7 @@
     n_tile, n_focus, strips, ker, nf,
     mask_hbm, class_ref, cell_ref, center_ref, w_hbm, wave_x_hbm, wave_y_hbm, right_hbm, left_hbm, down_hbm, along_hbm,
     ret_ref,
-    mask_v, sq_v, sp_v, out_v, in_v, hs_v, hr_v, zs_v, zr_v, shift_v, lit_v, raw_v, w_v, fil_v,
+    mask_v, sq_v, sp_v, out_v, in_v, hs_v, hr_v, zs_v, zr_v, shift_v, lit_v, raw_v, w_v, fil_v, xs_v,
     wave_x, wave_y, right_ref, left_ref, down_ref, along_ref,
     mask_sem, h_send, h_recv, z_send, z_recv, s_send, s_recv, r_send, r_recv, own_sem, table_sem,
 ):
@@ -127,19 +127,21 @@
     tables[0].wait()
     tables[1].wait()
 
-    def spectrum(t):
-        projected = jnp.dot(mask_v[t], wave_x[...], preferred_element_type=F32).astype(BF16)
-        raw = jnp.dot(whole(wave_y), projected, preferred_element_type=F32)
-        top, bottom = raw[:nf], pltpu.roll(raw[nf:], nf, 1)
-        real, imag = (top - bottom) / px, -(top + bottom) / px
+    batch = 4 if tiles % 4 == 0 else 1
+
+    def forward(step, carry):
+        masks = mask_v[pl.ds(step * batch, batch)].reshape(batch * px, px)
+        projected = jnp.dot(masks, wave_x[...], preferred_element_type=F32).astype(BF16)
+        beside = jnp.concatenate([projected[i * px : (i + 1) * px] for i in range(batch)], axis=1)
+        raws = jnp.dot(whole(wave_y), beside, preferred_element_type=F32)
         low = lax.broadcasted_iota(jnp.int32, (half, 2 * nf), 1) < nf
-        packed_re = jnp.where(low, real[:half], pltpu.roll(real[half:], nf, 1))
-        packed_im = jnp.where(low, pltpu.roll(imag[:half], nf, 1), imag[half:])
-        sp_v[t] = jnp.concatenate([packed_re, packed_im], axis=0).astype(BF16)
-
-    def forward(step, carry):
-        for i in range(2):
-            spectrum(2 * step + i)
+        for i in range(batch):
+            raw = raws[:, i * 2 * nf : (i + 1) * 2 * nf]
+            top, bottom = raw[:nf], pltpu.roll(raw[nf:], nf, 1)
+            real, imag = (top - bottom) / px, -(top + bottom) / px
+            packed_re = jnp.where(low, real[:half], pltpu.roll(real[half:], nf, 1))
+            packed_im = jnp.where(low, pltpu.roll(imag[:half], nf, 1), imag[half:])
+            sp_v[step * batch + i] = jnp.concatenate([packed_re, packed_im], axis=0).astype(BF16)
         return carry
 
     sums = sq_v[...]
@@ -211,7 +213,7 @@
 
     tables[2].wait()
     tables[3].wait()
-    lax.fori_loop(0, tiles // 2, forward, 0)
+    lax.fori_loop(0, tiles // batch, forward, 0)
 
     for o in range(1, n_focus):
         h_copy(o).wait_recv()
@@ -273,17 +275,20 @@
             rows.append(jnp.concatenate([kr * sr - ki * si, kr * si + ki * sr], axis=1).astype(BF16))
         return jnp.concatenate(rows, axis=0)
 
+    def sideways(which):
+        xs_v[which] = jnp.dot(fil_v[which], whole(right_ref), preferred_element_type=F32).astype(BF16)
+
     def image(now, after):
-        across = jnp.dot(fil_v[now], whole(right_ref), preferred_element_type=F32).astype(BF16)
+        sideways(1 - now)
         left = left_ref[...]
         total = jnp.zeros((Q, Q), F32)
         for first in range(0, ker, 4):
             sides = []
             for m in range(first, min(first + 4, ker)):
                 if m % 2 == 0:
-                    fil_v[1 - now, m * half : (m + 2) * half, :] = filtered(*after, m)
-                rows = across[m * half : (m + 1) * half]
-                sides.append(jnp.concatenate([rows[:, i * Q : (i + 1) * Q] for i in range(4)], axis=0))
+                    fil_v[now, m * half : (m + 2) * half, :] = filtered(*after, m)
+                sides.append(jnp.concatenate(
+                    [xs_v[now, m * half : (m + 1) * half, i * Q : (i + 1) * Q] for i in range(4)], axis=0))
             fields = jnp.dot(left, jnp.concatenate(sides, axis=1), preferred_element_type=F32)
             power = fields * fields
             for i in range(len(sides)):
@@ -294,18 +299,21 @@
     tables[5].wait()
     tables[6].wait()
     s_copy(1).wait_recv()
-    for k in range(0, ker, 2):
-        fil_v[0, k * half : (k + 2) * half, :] = filtered(1, 0, k)
+    for j in range(CAP):
+        for k in range(0, ker, 2):
+            fil_v[j, k * half : (k + 2) * half, :] = filtered(1, j, k)
+    sideways(0)
 
     def serve(step, carry):
         o = lax.rem(step + 1, n_focus)
         following = lax.rem(step + 2, n_focus)
+
+        @pl.when(step < n_focus - 2)
+        def _():
+            s_copy(following).wait_recv()
+
         for j in range(CAP):
-            if j == CAP - 1:
-                @pl.when(step < n_focus - 2)
-                def _():
-                    s_copy(following).wait_recv()
-            lit_v[o, j] = image(j % 2, (o, j + 1) if j < CAP - 1 else (following, 0))
+            lit_v[o, j] = image(j, (following, j))
 
         @pl.when(o != 0)
         def _():
@@ -392,7 +400,8 @@
             pltpu.VMEM((n_focus, CAP, Q, Q), BF16),
             pltpu.VMEM((ker, parts, area), BF16),
             pltpu.VMEM((ker, parts * half, 2 * nf), F32),
-            pltpu.VMEM((2, ker * half, 4 * nf), BF16),
+            pltpu.VMEM((CAP, ker * half, 4 * nf), BF16),
+            pltpu.VMEM((CAP, ker * half, 4 * Q), BF16),
         ] + [pltpu.VMEM(table.shape, table.dtype) for table in tables] + [
             dma((tiles,)),
             dma((n_focus,)), dma((n_focus,)),

time: 37.3 us -> 33.6 us (0.901)
  Pallas kernels: 37.2 us -> 33.5 us
    pallas_call x1, Pallas kernels: 32.7 us -> 29 us  [per_device(): pl.pallas_call(functools.partial(imaging_kernel, n_tile, n_focus, strips,...]
where the time goes in v4:
time: 33.6 us; the launch traced here: 33.5 us
  Pallas kernels  33.5 us (100%)
    pallas_call x1, Pallas kernels, per_device(): pl.pallas_call(functools.partial(imaging_kernel, n_tile, n_focus, strips,...  29 us
    pallas_call x1, Pallas kernels, per_device(): pl.pallas_call(resist_kernel, out_shape=jax.ShapeDtypeStruct((tiles, px,...  4.5 us

profile of v4, /device:TPU:0, one launch (start us, length us, event | category | flops | bytes accessed | tf_op | source)
XLA Modules:
  0.0 33.5 jit_solution(15694494297108777219)
XLA Ops:
  0.0 29.0 %imaging.1 = bf16[8,2,128,128]{3,2,1,0:T(8,128)(2,1)} custom-call(bf16[8,512,512]{2,1,0:T(8,128)(2,1)} %mask_hbm.1, s32[8]{0:T(128)} %bitcast.3, s32[8]{0:T(128)} %cell_ref.1, f32[8]{0:T(128)} %center_ref.1, bf16[1,24,4,4096]{3,2,1,0:T(4,128)(2,1)} %w_hbm.1, bf16[512,128]{1,0:T(8,128)(2,1)} %constant.16.clone.wave_x_hbm, ...), custom_call_target="tpu_custom_call" | custom-call | flops 6442450944 | bytes 8388608 | tf_op jit(solution)/shard_map/imaging/pallas_call | solution.py:384
  29.0 4.5 %resist.1 = bf16[8,512,512]{2,1,0:T(8,128)(2,1)} custom-call(s32[8]{0:T(128)} %bitcast.4, bf16[16,128,128]{2,1,0:T(8,128)(2,1)} %bitcast.2, bf16[4,128,128]{2,1,0:T(8,128)(2,1)} %constant.22.clone.wide_hbm, bf16[512,128]{1,0:T(8,128)(2,1)} %constant.23.clone.tall_hbm), custom_call_target="tpu_custom_call" | custom-call | flops 671088640 | bytes 4194304 | tf_op jit(solution)/shard_map/resist/pallas_call | solution.py:419
